TPU v7x, 32 devices: a whole 2x2x4 slice. The times are simulated.
32 devices in a mesh: gy: 8 (over z, core), gz: 4 (over y, x).
Axes of the slice: x: 2, y: 2, z: 4, core: 2. Of those that a mesh axis runs over, the one named last changes fastest.
Arguments:
- adjoint: float32 [5, 32, 1024, 256], P(None, 'gz', 'gy'), may hold values from -6 to 6
- speed: float32 [32, 1024, 256], P('gz', 'gy'), may hold values from 0.5 to 2
- x_derivative: float32 [256, 256], replicated, may hold values from -0.375 to 0.375
- y_operators: float32 [2, 1024, 1024], replicated, may hold values from -0.1875 to 0.1875
- coupling: float32 [3, 5, 5], replicated, may hold values from -2.5 to 2.5
Outputs:
- advanced: float32 [5, 32, 1024, 256], P(None, 'gz', 'gy')
All inputs are finite; a program needn't handle non-finite values.
Results may differ from a plain program's by a relative error of at most 0.0001.
Values sent between devices are 32-bit elements; how exact they have to be, the bound alone decides.
A program may use at most 128 MiB of HBM per device.

v0:
```python
import functools

import jax
import jax.numpy as jnp
from jax import lax
from jax.experimental import pallas as pl
from jax.experimental.pallas import tpu as pltpu
from jax.sharding import PartitionSpec as P

stencil = (0.8, -0.2, 4.0 / 105.0, -1.0 / 280.0)
viscous = 0.5
stepping = 0.5
MESH = pl.DeviceIdType.MESH
LANES = 128


def split(values):
    high = values.astype(jnp.bfloat16)
    low = (values - high.astype(jnp.float32)).astype(jnp.bfloat16)
    return high, low


def y_kernel(
    n, nz, adjoint, speed, y_ops, coupling, terms, halos,
    gath, speeds, op_stage, lhs, rhs_high, rhs_low, outgo,
    gather_send, gather_recv, forward_send, forward_recv, back_send, back_recv,
    speed_send, speed_recv, halo_send, halo_recv, local_sem, op_sem,
):
    fields, depth, rows, width = adjoint.shape
    half_n = n // 2
    workers = n // 4
    planes = depth // workers
    cuts = width // LANES
    chunks = planes * cuts
    me = lax.axis_index("gy")
    mz = lax.axis_index("gz")
    half = me // half_n
    mine = me - half * half_n
    base = half * half_n
    first_worker = base + (1 - half) * workers
    rank = me - first_worker
    is_worker = jnp.logical_and(rank >= 0, rank < workers)
    partner = me + (1 - 2 * half) * workers
    above, below = lax.rem(mz + 1, nz), lax.rem(mz + nz - 1, nz)
    extent = y_ops.shape[1]
    half_rows = extent // 2

    barrier = pltpu.get_barrier_semaphore()
    for side in (above, below):
        pl.semaphore_signal(barrier, inc=1, device_id=(me, side), device_id_type=MESH)

    @pl.when(is_worker)
    def _():
        def greet(i, carry):
            @pl.when(base + i != me)
            def _():
                pl.semaphore_signal(barrier, inc=1, device_id=(base + i, mz), device_id_type=MESH)
            return carry
        lax.fori_loop(0, half_n, greet, 0)
        pl.semaphore_signal(barrier, inc=1, device_id=(partner, mz), device_id_type=MESH)
        pl.semaphore_wait(barrier, half_n + 2)

    @pl.when(jnp.logical_not(is_worker))
    def _():
        def greet(i, carry):
            pl.semaphore_signal(barrier, inc=1, device_id=(first_worker + i, mz), device_id_type=MESH)
            return carry
        lax.fori_loop(0, workers, greet, 0)
        pl.semaphore_wait(barrier, workers + 2)

    def piece(ref, worker, chunk):
        plane = worker * planes + chunk // cuts
        lane = pl.multiple_of(lax.rem(chunk, cuts) * LANES, LANES)
        return ref.at[:, plane, :, pl.ds(lane, LANES)]

    def gather(worker, chunk):
        return pltpu.make_async_remote_copy(
            src_ref=piece(adjoint, worker, chunk), dst_ref=gath.at[chunk, me],
            send_sem=gather_send.at[worker, chunk], recv_sem=gather_recv.at[mine, chunk],
            device_id=(first_worker + worker, mz), device_id_type=MESH)

    def gathered(i, chunk):
        return pltpu.make_async_remote_copy(
            src_ref=gath.at[chunk, base + i], dst_ref=gath.at[chunk, base + i],
            send_sem=gather_send.at[0, chunk], recv_sem=gather_recv.at[i, chunk],
            device_id=(partner, mz), device_id_type=MESH)

    def forward(i, chunk):
        return pltpu.make_async_remote_copy(
            src_ref=gath.at[chunk, base + i], dst_ref=gath.at[chunk, base + i],
            send_sem=forward_send.at[i, chunk], recv_sem=forward_recv.at[i, chunk],
            device_id=(partner, mz), device_id_type=MESH)

    def forwarded(i, chunk):
        other = (1 - half) * half_n + i
        return pltpu.make_async_remote_copy(
            src_ref=gath.at[chunk, other], dst_ref=gath.at[chunk, other],
            send_sem=forward_send.at[i, chunk], recv_sem=forward_recv.at[i, chunk],
            device_id=(partner, mz), device_id_type=MESH)

    def own(chunk):
        return pltpu.make_async_copy(piece(adjoint, rank, chunk), gath.at[chunk, me], local_sem.at[chunk])

    def speed_copy(worker):
        return pltpu.make_async_remote_copy(
            src_ref=speed.at[pl.ds(worker * planes, planes)], dst_ref=speeds.at[mine],
            send_sem=speed_send.at[worker], recv_sem=speed_recv.at[mine],
            device_id=(first_worker + worker, mz), device_id_type=MESH)

    def speed_arrival(i):
        return pltpu.make_async_remote_copy(
            src_ref=speed.at[pl.ds(0, planes)], dst_ref=speeds.at[i],
            send_sem=speed_send.at[0], recv_sem=speed_recv.at[i],
            device_id=(partner, mz), device_id_type=MESH)

    def back(i, chunk, slot):
        return pltpu.make_async_remote_copy(
            src_ref=outgo.at[slot, i], dst_ref=piece(terms, rank, chunk),
            send_sem=back_send.at[i, slot], recv_sem=back_recv.at[rank, chunk],
            device_id=(base + i, mz), device_id_type=MESH)

    def back_own(chunk, slot):
        return pltpu.make_async_copy(
            outgo.at[slot, mine], piece(terms, rank, chunk), back_send.at[mine, slot])

    def back_arrival(worker, chunk):
        return pltpu.make_async_remote_copy(
            src_ref=outgo.at[0, 0], dst_ref=piece(terms, worker, chunk),
            send_sem=back_send.at[0, 0], recv_sem=back_recv.at[worker, chunk],
            device_id=(first_worker + worker, mz), device_id_type=MESH)

    reach = halos.shape[2]
    halo_up = pltpu.make_async_remote_copy(
        src_ref=adjoint.at[:, pl.ds(depth - reach, reach)], dst_ref=halos.at[0],
        send_sem=halo_send.at[0], recv_sem=halo_recv.at[0],
        device_id=(me, above), device_id_type=MESH)
    halo_down = pltpu.make_async_remote_copy(
        src_ref=adjoint.at[:, pl.ds(0, reach)], dst_ref=halos.at[1],
        send_sem=halo_send.at[1], recv_sem=halo_recv.at[1],
        device_id=(me, below), device_id_type=MESH)

    def each(count, body):
        def step(i, carry):
            body(i)
            return carry
        lax.fori_loop(0, count, step, 0)

    @pl.when(jnp.logical_not(is_worker))
    def _():
        def send(chunk):
            @pl.when(chunk >= 2)
            def _():
                each(workers, lambda w: gather(w, chunk - 2).wait_send())
            each(workers, lambda w: gather(w, chunk).start())

            @pl.when(chunk == 0)
            def _():
                each(workers, lambda w: speed_copy(w).start())
                halo_up.start()
                halo_down.start()
        each(chunks, send)
        for last in (chunks - 2, chunks - 1):
            each(workers, lambda w: gather(w, last).wait_send())
        each(workers, lambda w: speed_copy(w).wait_send())
        each(chunks, lambda c: each(workers, lambda w: back_arrival(w, c).wait_recv()))

    @pl.when(is_worker)
    def _():
        def to_mates(chunk):
            def one(w):
                @pl.when(w != rank)
                def _():
                    gather(w, chunk).start()
            each(workers, one)
            own(chunk).start()
        each(chunks, to_mates)

        def mates(fn):
            def one(w):
                @pl.when(w != rank)
                def _():
                    fn(w)
            each(workers, one)

        def others(fn):
            def one(i):
                @pl.when(i != mine)
                def _():
                    fn(i)
            each(half_n, one)

        mates(lambda w: speed_copy(w).start())
        own_speed = pltpu.make_async_copy(
            speed.at[pl.ds(rank * planes, planes)], speeds.at[mine], op_sem.at[1])
        own_speed.start()
        op_row = pl.multiple_of(half * half_rows, half_rows)
        op_copy = pltpu.make_async_copy(
            y_ops.at[:, pl.ds(op_row, half_rows)], op_stage, op_sem.at[0])
        op_copy.start()

        def send_forward(chunk):
            own(chunk).wait()
            forward(mine, chunk).start()

            def step(k):
                i = lax.rem(k + (1 - half) * workers, half_n)

                @pl.when(i != mine)
                def _():
                    gathered(i, chunk).wait_recv()
                    forward(i, chunk).start()
            each(half_n, step)

        send_forward(0)
        halo_up.start()
        halo_down.start()
        op_copy.wait()

        def prepare(i):
            top = pl.multiple_of(i * rows, rows)
            for op in range(2):
                high, low = split(op_stage[op, pl.ds(top, rows), :])
                lhs[i, op * rows:(op + 1) * rows, :] = high
                lhs[i, (2 + op) * rows:(3 + op) * rows, :] = low
        each(half_n, prepare)
        own_speed.wait()
        others(lambda i: speed_arrival(i).wait_recv())

        def work(chunk):
            @pl.when(chunk + 1 < chunks)
            def _():
                @pl.when(chunk >= 1)
                def _():
                    each(half_n, lambda i: forward(i, chunk - 1).wait_send())
                send_forward(chunk + 1)

            each(half_n, lambda i: forwarded(i, chunk).wait_recv())

            def convert(b):
                top = pl.multiple_of(b * rows, rows)
                for f in range(fields):
                    high, low = split(gath[chunk, b, f])
                    rhs_high[pl.ds(top, rows), f * LANES:(f + 1) * LANES] = high
                    rhs_low[pl.ds(top, rows), f * LANES:(f + 1) * LANES] = low
            each(n, convert)
            slot = lax.rem(chunk, 2)
            plane = chunk // cuts
            lane = pl.multiple_of(lax.rem(chunk, cuts) * LANES, LANES)

            @pl.when(chunk >= 2)
            def _():
                others(lambda i: back(i, chunk - 2, slot).wait_send())
                back_own(chunk - 2, slot).wait()

            def produce(k):
                i = k + half * (half_n - 1 - 2 * k)
                full = jnp.dot(lhs[i], rhs_high[...], preferred_element_type=jnp.float32)
                rest = jnp.dot(lhs[i, :2 * rows], rhs_low[...], preferred_element_type=jnp.float32)
                both = full[:2 * rows] + full[2 * rows:] + rest
                pace = speeds[i, plane, :, pl.ds(lane, LANES)]
                for f in range(fields):
                    total = coupling[1, 0, f] * both[:rows, :LANES]
                    for g in range(1, fields):
                        total = total + coupling[1, g, f] * both[:rows, g * LANES:(g + 1) * LANES]
                    outgo[slot, i, f] = pace * total + viscous * both[rows:, f * LANES:(f + 1) * LANES]

                @pl.when(i != mine)
                def _():
                    back(i, chunk, slot).start()

                @pl.when(i == mine)
                def _():
                    back_own(chunk, slot).start()
            each(half_n, produce)
        each(chunks, work)

        for last in (chunks - 2, chunks - 1):
            each(half_n, lambda i: forward(i, last).wait_send())
            others(lambda i: back(i, last, last % 2).wait_send())
            back_own(last, last % 2).wait()
        each(chunks, lambda c: mates(lambda w: gather(w, c).wait_send()))
        mates(lambda w: speed_copy(w).wait_send())
        each(chunks, lambda c: mates(lambda w: back_arrival(w, c).wait_recv()))

    halo_up.wait()
    halo_down.wait()


def local_kernel(adjoint, halos, speed, x_op, coupling, terms, out, ext, along):
    fields, depth, rows, width = adjoint.shape
    reach = len(stencil)
    ext[:, :reach] = halos[0]
    ext[:, reach:reach + depth] = adjoint[...]
    ext[:, reach + depth:] = halos[1]
    x_high, x_low = split(x_op[...])
    contract = (((1,), (1,)), ((), ()))

    def times(left, right):
        return lax.dot_general(left, right, contract, preferred_element_type=jnp.float32)

    for f in range(fields):
        high, low = split(adjoint[f].reshape(depth * rows, width))
        product = times(high, x_high) + times(high, x_low) + times(low, x_high)
        along[f] = product.reshape(depth, rows, width)

    def plane(p, carry):
        across = []
        for g in range(fields):
            total = None
            for step, weight in enumerate(stencil):
                part = weight * (ext[g, p + reach + step + 1] - ext[g, p + reach - step - 1])
                total = part if total is None else total + part
            across.append(total)
        pace = speed[p]
        for f in range(fields):
            total = coupling[0, 0, f] * along[0, p] + coupling[2, 0, f] * across[0]
            for g in range(1, fields):
                total = total + coupling[0, g, f] * along[g, p] + coupling[2, g, f] * across[g]
            out[f, p] = adjoint[f, p] + stepping * (pace * total + terms[f, p])
        return carry
    lax.fori_loop(0, depth, plane, 0)


def shards(n, nz, adjoint, speed, x_derivative, y_operators, coupling):
    fields, depth, rows, width = adjoint.shape
    half_n, workers = n // 2, n // 4
    planes = depth // workers
    chunks = planes * (width // LANES)
    reach = len(stencil)
    extent = y_operators.shape[1]
    f32, bf16 = jnp.float32, jnp.bfloat16
    dma = pltpu.SemaphoreType.DMA
    hbm = pl.BlockSpec(memory_space=pl.ANY)
    smem = pl.BlockSpec(memory_space=pltpu.SMEM)
    terms, halos = pl.pallas_call(
        functools.partial(y_kernel, n, nz),
        out_shape=(
            jax.ShapeDtypeStruct(adjoint.shape, f32),
            jax.ShapeDtypeStruct((2, fields, reach, rows, width), f32),
        ),
        in_specs=[hbm, hbm, hbm, smem],
        out_specs=(hbm, hbm),
        scratch_shapes=[
            pltpu.VMEM((chunks, n, fields, rows, LANES), f32),
            pltpu.VMEM((half_n, planes, rows, width), f32),
            pltpu.VMEM((2, extent // 2, extent), f32),
            pltpu.VMEM((half_n, 4 * rows, extent), bf16),
            pltpu.VMEM((extent, fields * LANES), bf16),
            pltpu.VMEM((extent, fields * LANES), bf16),
            pltpu.VMEM((2, half_n, fields, rows, LANES), f32),
            dma((workers, chunks)), dma((half_n, chunks)),
            dma((half_n, chunks)), dma((half_n, chunks)),
            dma((half_n, 2)), dma((workers, chunks)),
            dma((workers,)), dma((half_n,)),
            dma((2,)), dma((2,)), dma((chunks,)), dma((2,)),
        ],
        compiler_params=pltpu.CompilerParams(
            collective_id=0, has_side_effects=True, vmem_limit_bytes=56 * 2**20),
        cost_estimate=pl.CostEstimate(
            flops=12 * fields * depth * rows * width * extent,
            bytes_accessed=16 * fields * depth * rows * width, transcendentals=0),
    )(adjoint, speed, y_operators, coupling)

    tile = 16
    block = pl.BlockSpec((fields, depth, tile, width), lambda i: (0, 0, i, 0))
    return pl.pallas_call(
        local_kernel,
        grid=(rows // tile,),
        out_shape=jax.ShapeDtypeStruct(adjoint.shape, f32),
        in_specs=[
            block,
            pl.BlockSpec((2, fields, reach, tile, width), lambda i: (0, 0, 0, i, 0)),
            pl.BlockSpec((depth, tile, width), lambda i: (0, i, 0)),
            pl.BlockSpec((width, width), lambda i: (0, 0)),
            smem,
            block,
        ],
        out_specs=block,
        scratch_shapes=[
            pltpu.VMEM((fields, depth + 2 * reach, tile, width), f32),
            pltpu.VMEM((fields, depth, tile, width), f32),
        ],
        compiler_params=pltpu.CompilerParams(vmem_limit_bytes=40 * 2**20),
        cost_estimate=pl.CostEstimate(
            flops=6 * fields * depth * rows * width * width,
            bytes_accessed=20 * fields * depth * rows * width, transcendentals=0),
    )(adjoint, halos, speed, x_derivative, coupling, terms)


def solution(mesh):
    placed = (P(None, "gz", "gy", None), P("gz", "gy", None), P(), P(), P())
    body = functools.partial(shards, mesh.shape["gy"], mesh.shape["gz"])
    return jax.shard_map(
        body, mesh=mesh, in_specs=placed, out_specs=P(None, "gz", "gy", None), check_vma=False
    )
```

profile of v0, /device:TPU:1, one launch (start us, length us, event | category | flops | bytes accessed | tf_op | source)
XLA Modules:
  0.0 272.9 jit_solution(4998245883166105041)
XLA Ops:
  0.0 1.3 copy.6.coupling
  1.3 0.0 copy-start
  1.3 0.0 copy-start.2
  1.3 0.0 copy-start.3
  1.3 0.0 copy-start.4
  1.3 250.8 %shard_map.55 = (f32[5,8,128,256]{3,2,1,0:T(8,128)}, f32[2,5,4,128,256]{4,3,2,1,0:T(8,128)}) custom-call(f32[5,8,128,256]{3,2,1,0:T(8,128)} %adjoint.3, f32[8,128,256]{2,1,0:T(8,128)} %speed.3, f32[2,1024,1024]{2,1,0:T(8,128)} %y_ops.1, f32[3,5,5]{2,1,0:T(8,128)} %copy.6.coupling), custom_call_target="tpu_custom_call" | custom-call | flops 16106127360 | bytes 20971520 | tf_op jit(solution)/shard_map/pallas_call | solution.py:335
  252.1 0.0 copy-done
  252.1 0.0 copy-done.2
  252.2 0.0 copy-done.3
  252.2 0.0 copy-done.4
  252.2 0.0 copy-start.1
  252.2 2.5 copy-done.1
  254.7 18.3 %shard_map.56 = f32[5,8,128,256]{3,2,1,0:T(8,128)} custom-call(f32[5,8,128,256]{3,2,1,0:T(8,128)S(1)} %copy-done, f32[2,5,4,128,256]{4,3,2,1,0:T(8,128)S(1)} %copy-done.1, f32[8,128,256]{2,1,0:T(8,128)S(1)} %copy-done.2, f32[256,256]{1,0:T(8,128)S(1)} %copy-done.3, f32[3,5,5]{2,1,0:T(8,128)S(1)} %copy-done.4, f32[5,8,128,256]{3,2,1,0:T(8,128)} %get-tuple-element.8.terms), custom_call_target="tpu_custom_call" | custom-call | flops 2013265920 | bytes 26214400 | tf_op jit(solution)/shard_map/pallas_call | solution.py:366
Async XLA Ops:
  1.3 250.8 %copy-start = (f32[5,8,128,256]{3,2,1,0:T(8,128)S(1)}, f32[5,8,128,256]{3,2,1,0:T(8,128)}, u32[]{:S(2)}) copy-start(f32[5,8,128,256]{3,2,1,0:T(8,128)} %adjoint.3) | copy-start | bytes 15728644
  1.3 250.8 %copy-start.2 = (f32[8,128,256]{2,1,0:T(8,128)S(1)}, f32[8,128,256]{2,1,0:T(8,128)}, u32[]{:S(2)}) copy-start(f32[8,128,256]{2,1,0:T(8,128)} %speed.3) | copy-start | bytes 3145732
  1.3 250.8 %copy-start.3 = (f32[256,256]{1,0:T(8,128)S(1)}, f32[256,256]{1,0:T(8,128)}, u32[]{:S(2)}) copy-start(f32[256,256]{1,0:T(8,128)} %x_op.1) | copy-start | bytes 786436
  1.3 250.9 %copy-start.4 = (f32[3,5,5]{2,1,0:T(8,128)S(1)}, f32[3,5,5]{2,1,0:T(8,128)}, u32[]{:S(2)}) copy-start(f32[3,5,5]{2,1,0:T(8,128)} %copy.6.coupling) | copy-start | bytes 904
  252.2 2.5 copy-start.1
where the time goes:
time: 273 us
  Pallas kernels  269 us (99%)
  local copies, waits for them, and re-layouts  3.8 us (1%)
    pallas_call x1, Pallas kernels, shards(): pl.pallas_call(functools.partial(y_kernel, n, nz), out_shape=(jax.ShapeDt...  251 us
    pallas_call x1, Pallas kernels, shards(): pl.pallas_call(local_kernel, grid=(rows // tile,), out_shape=jax.ShapeDty...  18.3 us

commit v1 on v0

--- a/solution.py
+++ b/solution.py
@@ -12,6 +12,7 @@
 stepping = 0.5
 MESH = pl.DeviceIdType.MESH
 LANES = 128
+TILE = 16
 
 
 def split(values):
@@ -21,10 +22,11 @@
 
 
 def y_kernel(
-    n, nz, adjoint, speed, y_ops, coupling, terms, halos,
+    n, nz, adjoint, speed, y_ops, x_op, coupling, terms, halos, local,
     gath, speeds, op_stage, lhs, rhs_high, rhs_low, outgo,
+    x_mat, ext, along, pace_tile, result,
     gather_send, gather_recv, forward_send, forward_recv, back_send, back_recv,
-    speed_send, speed_recv, halo_send, halo_recv, local_sem, op_sem,
+    speed_send, speed_recv, halo_send, halo_recv, local_sem, op_sem, tile_sem,
 ):
     fields, depth, rows, width = adjoint.shape
     half_n = n // 2
@@ -145,6 +147,33 @@
             return carry
         lax.fori_loop(0, count, step, 0)
 
+    x_copy = pltpu.make_async_copy(x_op, x_mat, tile_sem.at[0])
+    tiles = rows // TILE
+    local_steps = max(1, chunks // 2)
+    per_step = -(-tiles // local_steps)
+
+    def arrive():
+        x_copy.wait()
+        halo_up.wait_recv()
+        halo_down.wait_recv()
+
+    def local_tile(t):
+        strip = pl.ds(pl.multiple_of(t * TILE, TILE), TILE)
+        moves = [
+            pltpu.make_async_copy(halos.at[0, :, :, strip, :], ext.at[:, pl.ds(0, reach)], tile_sem.at[1]),
+            pltpu.make_async_copy(adjoint.at[:, :, strip, :], ext.at[:, pl.ds(reach, depth)], tile_sem.at[2]),
+            pltpu.make_async_copy(halos.at[1, :, :, strip, :], ext.at[:, pl.ds(reach + depth, reach)], tile_sem.at[3]),
+            pltpu.make_async_copy(speed.at[:, strip, :], pace_tile, tile_sem.at[4]),
+        ]
+        for move in moves:
+            move.start()
+        for move in moves:
+            move.wait()
+        local_terms(x_mat, ext, along, pace_tile, coupling, result)
+        store = pltpu.make_async_copy(result, local.at[:, :, strip, :], tile_sem.at[5])
+        store.start()
+        store.wait()
+
     @pl.when(jnp.logical_not(is_worker))
     def _():
         def send(chunk):
@@ -158,7 +187,10 @@
                 each(workers, lambda w: speed_copy(w).start())
                 halo_up.start()
                 halo_down.start()
+                x_copy.start()
         each(chunks, send)
+        arrive()
+        each(tiles, local_tile)
         for last in (chunks - 2, chunks - 1):
             each(workers, lambda w: gather(w, last).wait_send())
         each(workers, lambda w: speed_copy(w).wait_send())
@@ -214,6 +246,7 @@
         send_forward(0)
         halo_up.start()
         halo_down.start()
+        x_copy.start()
         op_copy.wait()
 
         def prepare(i):
@@ -259,10 +292,11 @@
                 both = full[:2 * rows] + full[2 * rows:] + rest
                 pace = speeds[i, plane, :, pl.ds(lane, LANES)]
                 for f in range(fields):
-                    total = coupling[1, 0, f] * both[:rows, :LANES]
+                    total = coupling[0, 1, f] * both[:rows, :LANES]
                     for g in range(1, fields):
-                        total = total + coupling[1, g, f] * both[:rows, g * LANES:(g + 1) * LANES]
-                    outgo[slot, i, f] = pace * total + viscous * both[rows:, f * LANES:(f + 1) * LANES]
+                        total = total + coupling[g, 1, f] * both[:rows, g * LANES:(g + 1) * LANES]
+                    outgo[slot, i, f] = (stepping * pace) * total + (
+                        stepping * viscous) * both[rows:, f * LANES:(f + 1) * LANES]
 
                 @pl.when(i != mine)
                 def _():
@@ -272,6 +306,20 @@
                 def _():
                     back_own(chunk, slot).start()
             each(half_n, produce)
+
+            @pl.when(chunk == chunks - 1 - local_steps)
+            def _():
+                arrive()
+
+            @pl.when(jnp.logical_and(chunk >= chunks - 1 - local_steps, chunk < chunks - 1))
+            def _():
+                first = (chunk - (chunks - 1 - local_steps)) * per_step
+
+                def one(k):
+                    @pl.when(first + k < tiles)
+                    def _():
+                        local_tile(first + k)
+                each(per_step, one)
         each(chunks, work)
 
         for last in (chunks - 2, chunks - 1):
@@ -282,26 +330,23 @@
         mates(lambda w: speed_copy(w).wait_send())
         each(chunks, lambda c: mates(lambda w: back_arrival(w, c).wait_recv()))
 
-    halo_up.wait()
-    halo_down.wait()
-
-
-def local_kernel(adjoint, halos, speed, x_op, coupling, terms, out, ext, along):
-    fields, depth, rows, width = adjoint.shape
+    halo_up.wait_send()
+    halo_down.wait_send()
+
+
+def local_terms(x_mat, ext, along, pace_tile, coupling, result):
+    fields, depth, tile, width = result.shape
     reach = len(stencil)
-    ext[:, :reach] = halos[0]
-    ext[:, reach:reach + depth] = adjoint[...]
-    ext[:, reach + depth:] = halos[1]
-    x_high, x_low = split(x_op[...])
+    x_high, x_low = split(x_mat[...])
     contract = (((1,), (1,)), ((), ()))
 
     def times(left, right):
         return lax.dot_general(left, right, contract, preferred_element_type=jnp.float32)
 
     for f in range(fields):
-        high, low = split(adjoint[f].reshape(depth * rows, width))
+        high, low = split(ext[f, reach:reach + depth].reshape(depth * tile, width))
         product = times(high, x_high) + times(high, x_low) + times(low, x_high)
-        along[f] = product.reshape(depth, rows, width)
+        along[f] = product.reshape(depth, tile, width)
 
     def plane(p, carry):
         across = []
@@ -311,12 +356,12 @@
                 part = weight * (ext[g, p + reach + step + 1] - ext[g, p + reach - step - 1])
                 total = part if total is None else total + part
             across.append(total)
-        pace = speed[p]
+        pace = stepping * pace_tile[p]
         for f in range(fields):
-            total = coupling[0, 0, f] * along[0, p] + coupling[2, 0, f] * across[0]
+            total = coupling[0, 0, f] * along[0, p] + coupling[0, 2, f] * across[0]
             for g in range(1, fields):
-                total = total + coupling[0, g, f] * along[g, p] + coupling[2, g, f] * across[g]
-            out[f, p] = adjoint[f, p] + stepping * (pace * total + terms[f, p])
+                total = total + coupling[g, 0, f] * along[g, p] + coupling[g, 2, f] * across[g]
+            result[f, p] = ext[f, p + reach] + pace * total
         return carry
     lax.fori_loop(0, depth, plane, 0)
 
@@ -332,14 +377,15 @@
     dma = pltpu.SemaphoreType.DMA
     hbm = pl.BlockSpec(memory_space=pl.ANY)
     smem = pl.BlockSpec(memory_space=pltpu.SMEM)
-    terms, halos = pl.pallas_call(
+    terms, halos, local = pl.pallas_call(
         functools.partial(y_kernel, n, nz),
         out_shape=(
             jax.ShapeDtypeStruct(adjoint.shape, f32),
             jax.ShapeDtypeStruct((2, fields, reach, rows, width), f32),
+            jax.ShapeDtypeStruct(adjoint.shape, f32),
         ),
-        in_specs=[hbm, hbm, hbm, smem],
-        out_specs=(hbm, hbm),
+        in_specs=[hbm, hbm, hbm, hbm, smem],
+        out_specs=(hbm, hbm, hbm),
         scratch_shapes=[
             pltpu.VMEM((chunks, n, fields, rows, LANES), f32),
             pltpu.VMEM((half_n, planes, rows, width), f32),
@@ -348,43 +394,24 @@
             pltpu.VMEM((extent, fields * LANES), bf16),
             pltpu.VMEM((extent, fields * LANES), bf16),
             pltpu.VMEM((2, half_n, fields, rows, LANES), f32),
+            pltpu.VMEM((width, width), f32),
+            pltpu.VMEM((fields, depth + 2 * reach, TILE, width), f32),
+            pltpu.VMEM((fields, depth, TILE, width), f32),
+            pltpu.VMEM((depth, TILE, width), f32),
+            pltpu.VMEM((fields, depth, TILE, width), f32),
             dma((workers, chunks)), dma((half_n, chunks)),
             dma((half_n, chunks)), dma((half_n, chunks)),
             dma((half_n, 2)), dma((workers, chunks)),
             dma((workers,)), dma((half_n,)),
-            dma((2,)), dma((2,)), dma((chunks,)), dma((2,)),
+            dma((2,)), dma((2,)), dma((chunks,)), dma((2,)), dma((6,)),
         ],
         compiler_params=pltpu.CompilerParams(
             collective_id=0, has_side_effects=True, vmem_limit_bytes=56 * 2**20),
         cost_estimate=pl.CostEstimate(
             flops=12 * fields * depth * rows * width * extent,
             bytes_accessed=16 * fields * depth * rows * width, transcendentals=0),
-    )(adjoint, speed, y_operators, coupling)
-
-    tile = 16
-    block = pl.BlockSpec((fields, depth, tile, width), lambda i: (0, 0, i, 0))
-    return pl.pallas_call(
-        local_kernel,
-        grid=(rows // tile,),
-        out_shape=jax.ShapeDtypeStruct(adjoint.shape, f32),
-        in_specs=[
-            block,
-            pl.BlockSpec((2, fields, reach, tile, width), lambda i: (0, 0, 0, i, 0)),
-            pl.BlockSpec((depth, tile, width), lambda i: (0, i, 0)),
-            pl.BlockSpec((width, width), lambda i: (0, 0)),
-            smem,
-            block,
-        ],
-        out_specs=block,
-        scratch_shapes=[
-            pltpu.VMEM((fields, depth + 2 * reach, tile, width), f32),
-            pltpu.VMEM((fields, depth, tile, width), f32),
-        ],
-        compiler_params=pltpu.CompilerParams(vmem_limit_bytes=40 * 2**20),
-        cost_estimate=pl.CostEstimate(
-            flops=6 * fields * depth * rows * width * width,
-            bytes_accessed=20 * fields * depth * rows * width, transcendentals=0),
-    )(adjoint, halos, speed, x_derivative, coupling, terms)
+    )(adjoint, speed, y_operators, x_derivative, jnp.transpose(coupling, (1, 0, 2)))
+    return local + terms
 
 
 def solution(mesh):

time: 273 us -> 258 us (0.945)
  Pallas kernels: 269 us -> 251 us
  other arithmetic: 0 us -> 7.36 us
  local copies, waits for them, and re-layouts: 3.8 us -> 0 us
    pallas_call x1 -> x0, Pallas kernels: 18.3 us -> none  [shards(): pl.pallas_call(local_kernel, grid=(rows // tile,), out_shape=jax.ShapeDty...]
    add x0 -> x1, other arithmetic: none -> 7.36 us  [shards(): return local + terms]
    unnamed x11 -> x0, local copies, waits for them, and re-layouts: 3.8 us -> none
where the time goes in v1:
time: 258 us
  Pallas kernels  251 us (97%)
  other arithmetic  7.36 us (3%)
    pallas_call x1, Pallas kernels, shards(): pl.pallas_call(functools.partial(y_kernel, n, nz), out_shape=(jax.ShapeDt...  251 us
    add x1, other arithmetic, shards(): return local + terms  7.36 us

profile of v1, /device:TPU:1, one launch (start us, length us, event | category | flops | bytes accessed | tf_op | source)
XLA Modules:
  0.0 258.0 jit_solution(9382187161350012546)
XLA Ops:
  0.0 250.7 %shard_map.55 = (f32[5,8,128,256]{3,2,1,0:T(8,128)}, f32[2,5,4,128,256]{4,3,2,1,0:T(8,128)}, f32[5,8,128,256]{3,2,1,0:T(8,128)}) custom-call(f32[5,8,128,256]{3,2,1,0:T(8,128)} %adjoint.1, f32[8,128,256]{2,1,0:T(8,128)} %speed.1, f32[2,1024,1024]{2,1,0:T(8,128)} %y_ops.1, f32[256,256]{1,0:T(8,128)} %x_op.1, f32[5,3,5]{2,1,0:T(4,128)} %bitcast.1), custom_call_target="tpu_custom_call" | custom-call | flops 16106127360 | bytes 20971520 | tf_op jit(solution)/shard_map/pallas_call | solution.py:380
  250.7 7.4 %add.3 = f32[5,8,128,256]{3,2,1,0:T(8,128)} add(f32[5,8,128,256]{3,2,1,0:T(8,128)} %get-tuple-element.7, f32[5,8,128,256]{3,2,1,0:T(8,128)} %get-tuple-element.8) | non-fusion elementwise | flops 1310720 | bytes 15728640 | tf_op jit(solution)/shard_map/add | solution.py:414

commit v2 on v1

--- a/solution.py
+++ b/solution.py
@@ -22,11 +22,11 @@
 
 
 def y_kernel(
-    n, nz, adjoint, speed, y_ops, x_op, coupling, terms, halos, local,
+    n, nz, adjoint, speed, y_ops, x_op, coupling, out, halos,
     gath, speeds, op_stage, lhs, rhs_high, rhs_low, outgo,
-    x_mat, ext, along, pace_tile, result,
+    x_mat, ext, along, pace_tile, terms, total_terms,
     gather_send, gather_recv, forward_send, forward_recv, back_send, back_recv,
-    speed_send, speed_recv, halo_send, halo_recv, local_sem, op_sem, tile_sem,
+    speed_send, speed_recv, halo_send, halo_recv, local_sem, op_sem, tile_sem, out_sem,
 ):
     fields, depth, rows, width = adjoint.shape
     half_n = n // 2
@@ -100,19 +100,29 @@
             send_sem=forward_send.at[i, chunk], recv_sem=forward_recv.at[i, chunk],
             device_id=(partner, mz), device_id_type=MESH)
 
+    def forward_mine(chunk):
+        return pltpu.make_async_remote_copy(
+            src_ref=piece(adjoint, rank, chunk), dst_ref=gath.at[chunk, me],
+            send_sem=forward_send.at[mine, chunk], recv_sem=forward_recv.at[mine, chunk],
+            device_id=(partner, mz), device_id_type=MESH)
+
     def own(chunk):
         return pltpu.make_async_copy(piece(adjoint, rank, chunk), gath.at[chunk, me], local_sem.at[chunk])
 
-    def speed_copy(worker):
-        return pltpu.make_async_remote_copy(
-            src_ref=speed.at[pl.ds(worker * planes, planes)], dst_ref=speeds.at[mine],
-            send_sem=speed_send.at[worker], recv_sem=speed_recv.at[mine],
+    def speed_piece(ref, plane, chunk):
+        lane = pl.multiple_of(lax.rem(chunk, cuts) * LANES, LANES)
+        return ref.at[plane + chunk // cuts, :, pl.ds(lane, LANES)]
+
+    def speed_copy(worker, chunk):
+        return pltpu.make_async_remote_copy(
+            src_ref=speed_piece(speed, worker * planes, chunk), dst_ref=speed_piece(speeds.at[mine], 0, chunk),
+            send_sem=speed_send.at[worker, chunk], recv_sem=speed_recv.at[mine, chunk],
             device_id=(first_worker + worker, mz), device_id_type=MESH)
 
-    def speed_arrival(i):
-        return pltpu.make_async_remote_copy(
-            src_ref=speed.at[pl.ds(0, planes)], dst_ref=speeds.at[i],
-            send_sem=speed_send.at[0], recv_sem=speed_recv.at[i],
+    def speed_arrival(i, chunk):
+        return pltpu.make_async_remote_copy(
+            src_ref=speed_piece(speed, 0, chunk), dst_ref=speed_piece(speeds.at[i], 0, chunk),
+            send_sem=speed_send.at[0, chunk], recv_sem=speed_recv.at[i, chunk],
             device_id=(partner, mz), device_id_type=MESH)
 
     def back(i, chunk, slot):
@@ -132,14 +142,18 @@
             device_id=(first_worker + worker, mz), device_id_type=MESH)
 
     reach = halos.shape[2]
-    halo_up = pltpu.make_async_remote_copy(
-        src_ref=adjoint.at[:, pl.ds(depth - reach, reach)], dst_ref=halos.at[0],
-        send_sem=halo_send.at[0], recv_sem=halo_recv.at[0],
-        device_id=(me, above), device_id_type=MESH)
-    halo_down = pltpu.make_async_remote_copy(
-        src_ref=adjoint.at[:, pl.ds(0, reach)], dst_ref=halos.at[1],
-        send_sem=halo_send.at[1], recv_sem=halo_recv.at[1],
-        device_id=(me, below), device_id_type=MESH)
+
+    def halo_up(f):
+        return pltpu.make_async_remote_copy(
+            src_ref=adjoint.at[f, pl.ds(depth - reach, reach)], dst_ref=halos.at[0, f],
+            send_sem=halo_send.at[0, f], recv_sem=halo_recv.at[0, f],
+            device_id=(me, above), device_id_type=MESH)
+
+    def halo_down(f):
+        return pltpu.make_async_remote_copy(
+            src_ref=adjoint.at[f, pl.ds(0, reach)], dst_ref=halos.at[1, f],
+            send_sem=halo_send.at[1, f], recv_sem=halo_recv.at[1, f],
+            device_id=(me, below), device_id_type=MESH)
 
     def each(count, body):
         def step(i, carry):
@@ -147,6 +161,16 @@
             return carry
         lax.fori_loop(0, count, step, 0)
 
+    def halo_part(step):
+        def one(k):
+            f = 2 * step + k
+
+            @pl.when(f < fields)
+            def _():
+                halo_up(f).start()
+                halo_down(f).start()
+        each(2, one)
+
     x_copy = pltpu.make_async_copy(x_op, x_mat, tile_sem.at[0])
     tiles = rows // TILE
     local_steps = max(1, chunks // 2)
@@ -154,8 +178,8 @@
 
     def arrive():
         x_copy.wait()
-        halo_up.wait_recv()
-        halo_down.wait_recv()
+        each(fields, lambda f: halo_up(f).wait_recv())
+        each(fields, lambda f: halo_down(f).wait_recv())
 
     def local_tile(t):
         strip = pl.ds(pl.multiple_of(t * TILE, TILE), TILE)
@@ -169,32 +193,51 @@
             move.start()
         for move in moves:
             move.wait()
-        local_terms(x_mat, ext, along, pace_tile, coupling, result)
-        store = pltpu.make_async_copy(result, local.at[:, :, strip, :], tile_sem.at[5])
-        store.start()
-        store.wait()
+        local_terms(x_mat, ext, along, pace_tile, coupling, total_terms, t * TILE)
+
+    def store(worker, chunk):
+        return pltpu.make_async_copy(
+            piece(total_terms, worker, chunk), piece(out, worker, chunk), out_sem.at[worker, chunk])
+
+    def finish(worker, chunk):
+        plane = worker * planes + chunk // cuts
+        lanes = pl.ds(pl.multiple_of(lax.rem(chunk, cuts) * LANES, LANES), LANES)
+        for f in range(fields):
+            total_terms[f, plane, :, lanes] += terms[f, plane, :, lanes]
+        store(worker, chunk).start()
 
     @pl.when(jnp.logical_not(is_worker))
     def _():
         def send(chunk):
-            @pl.when(chunk >= 2)
+            @pl.when(chunk >= 3)
             def _():
                 each(workers, lambda w: gather(w, chunk - 2).wait_send())
             each(workers, lambda w: gather(w, chunk).start())
-
-            @pl.when(chunk == 0)
-            def _():
-                each(workers, lambda w: speed_copy(w).start())
-                halo_up.start()
-                halo_down.start()
-                x_copy.start()
-        each(chunks, send)
+            each(workers, lambda w: speed_copy(w, chunk).start())
+
+            @pl.when(chunk <= (fields + 1) // 2)
+            def _():
+                halo_part(chunk - 1)
+        x_copy.start()
+
+        def first(w):
+            gather(w, 0).start()
+            gather(w, 0).wait_send()
+        each(workers, first)
+        each(workers, lambda w: speed_copy(w, 0).start())
+        each(chunks - 1, lambda c: send(c + 1))
         arrive()
         each(tiles, local_tile)
         for last in (chunks - 2, chunks - 1):
             each(workers, lambda w: gather(w, last).wait_send())
-        each(workers, lambda w: speed_copy(w).wait_send())
-        each(chunks, lambda c: each(workers, lambda w: back_arrival(w, c).wait_recv()))
+        each(chunks, lambda c: each(workers, lambda w: speed_copy(w, c).wait_send()))
+
+        def collect(c):
+            def one(w):
+                back_arrival(w, c).wait_recv()
+                finish(w, c)
+            each(workers, one)
+        each(chunks, collect)
 
     @pl.when(is_worker)
     def _():
@@ -203,9 +246,9 @@
                 @pl.when(w != rank)
                 def _():
                     gather(w, chunk).start()
+                    speed_copy(w, chunk).start()
             each(workers, one)
             own(chunk).start()
-        each(chunks, to_mates)
 
         def mates(fn):
             def one(w):
@@ -221,32 +264,38 @@
                     fn(i)
             each(half_n, one)
 
-        mates(lambda w: speed_copy(w).start())
         own_speed = pltpu.make_async_copy(
             speed.at[pl.ds(rank * planes, planes)], speeds.at[mine], op_sem.at[1])
-        own_speed.start()
         op_row = pl.multiple_of(half * half_rows, half_rows)
         op_copy = pltpu.make_async_copy(
             y_ops.at[:, pl.ds(op_row, half_rows)], op_stage, op_sem.at[0])
-        op_copy.start()
 
         def send_forward(chunk):
-            own(chunk).wait()
-            forward(mine, chunk).start()
-
             def step(k):
                 i = lax.rem(k + (1 - half) * workers, half_n)
 
                 @pl.when(i != mine)
                 def _():
-                    gathered(i, chunk).wait_recv()
+                    @pl.when(jnp.logical_or(chunk > 0, rank == 0))
+                    def _():
+                        gathered(i, chunk).wait_recv()
                     forward(i, chunk).start()
             each(half_n, step)
 
+        to_mates(0)
+
+        @pl.when(rank > 0)
+        def _():
+            others(lambda i: gathered(i, 0).wait_recv())
+        forward_mine(0).start()
+        own_speed.start()
+        op_copy.start()
+        x_copy.start()
         send_forward(0)
-        halo_up.start()
-        halo_down.start()
-        x_copy.start()
+        to_mates(1)
+        forward_mine(1).start()
+        send_forward(1)
+        to_mates(2)
         op_copy.wait()
 
         def prepare(i):
@@ -257,17 +306,42 @@
                 lhs[i, (2 + op) * rows:(3 + op) * rows, :] = low
         each(half_n, prepare)
         own_speed.wait()
-        others(lambda i: speed_arrival(i).wait_recv())
+
+        def finish_all(c):
+            def one(w):
+                @pl.when(w != rank)
+                def _():
+                    back_arrival(w, c).wait_recv()
+                finish(w, c)
+            each(workers, one)
 
         def work(chunk):
-            @pl.when(chunk + 1 < chunks)
+            @pl.when(chunk + 2 < chunks)
             def _():
                 @pl.when(chunk >= 1)
                 def _():
                     each(half_n, lambda i: forward(i, chunk - 1).wait_send())
-                send_forward(chunk + 1)
-
-            each(half_n, lambda i: forwarded(i, chunk).wait_recv())
+                forward_mine(chunk + 2).start()
+                send_forward(chunk + 2)
+
+            @pl.when(chunk + 3 < chunks)
+            def _():
+                to_mates(chunk + 3)
+
+            @pl.when(chunk < (fields + 1) // 2)
+            def _():
+                halo_part(chunk)
+
+            slot = lax.rem(chunk, 2)
+
+            @pl.when(chunk >= 2)
+            def _():
+                others(lambda i: back(i, chunk - 2, slot).wait_send())
+                back_own(chunk - 2, slot).wait()
+
+            @pl.when(chunk == chunks - 1)
+            def _():
+                each(chunks - 2, finish_all)
 
             def convert(b):
                 top = pl.multiple_of(b * rows, rows)
@@ -275,15 +349,17 @@
                     high, low = split(gath[chunk, b, f])
                     rhs_high[pl.ds(top, rows), f * LANES:(f + 1) * LANES] = high
                     rhs_low[pl.ds(top, rows), f * LANES:(f + 1) * LANES] = low
-            each(n, convert)
-            slot = lax.rem(chunk, 2)
+            own(chunk).wait()
+            each(half_n, lambda i: convert(base + i))
+
+            def receive(k):
+                i = lax.rem(k + half * workers, half_n)
+                forwarded(i, chunk).wait_recv()
+                convert((1 - half) * half_n + i)
+            each(half_n, receive)
+            others(lambda i: speed_arrival(i, chunk).wait_recv())
             plane = chunk // cuts
             lane = pl.multiple_of(lax.rem(chunk, cuts) * LANES, LANES)
-
-            @pl.when(chunk >= 2)
-            def _():
-                others(lambda i: back(i, chunk - 2, slot).wait_send())
-                back_own(chunk - 2, slot).wait()
 
             def produce(k):
                 i = k + half * (half_n - 1 - 2 * k)
@@ -322,20 +398,23 @@
                 each(per_step, one)
         each(chunks, work)
 
+        each(half_n, lambda i: forward(i, chunks - 3).wait_send())
         for last in (chunks - 2, chunks - 1):
             each(half_n, lambda i: forward(i, last).wait_send())
             others(lambda i: back(i, last, last % 2).wait_send())
             back_own(last, last % 2).wait()
         each(chunks, lambda c: mates(lambda w: gather(w, c).wait_send()))
-        mates(lambda w: speed_copy(w).wait_send())
-        each(chunks, lambda c: mates(lambda w: back_arrival(w, c).wait_recv()))
-
-    halo_up.wait_send()
-    halo_down.wait_send()
-
-
-def local_terms(x_mat, ext, along, pace_tile, coupling, result):
-    fields, depth, tile, width = result.shape
+        each(chunks, lambda c: mates(lambda w: speed_copy(w, c).wait_send()))
+        finish_all(chunks - 2)
+        finish_all(chunks - 1)
+
+    each(chunks, lambda c: each(workers, lambda w: store(w, c).wait()))
+    each(fields, lambda f: halo_up(f).wait_send())
+    each(fields, lambda f: halo_down(f).wait_send())
+
+
+def local_terms(x_mat, ext, along, pace_tile, coupling, result, top):
+    fields, depth, tile, width = along.shape
     reach = len(stencil)
     x_high, x_low = split(x_mat[...])
     contract = (((1,), (1,)), ((), ()))
@@ -361,7 +440,7 @@
             total = coupling[0, 0, f] * along[0, p] + coupling[0, 2, f] * across[0]
             for g in range(1, fields):
                 total = total + coupling[g, 0, f] * along[g, p] + coupling[g, 2, f] * across[g]
-            result[f, p] = ext[f, p + reach] + pace * total
+            result[f, p, pl.ds(pl.multiple_of(top, tile), tile), :] = ext[f, p + reach] + pace * total
         return carry
     lax.fori_loop(0, depth, plane, 0)
 
@@ -377,15 +456,14 @@
     dma = pltpu.SemaphoreType.DMA
     hbm = pl.BlockSpec(memory_space=pl.ANY)
     smem = pl.BlockSpec(memory_space=pltpu.SMEM)
-    terms, halos, local = pl.pallas_call(
+    out, _ = pl.pallas_call(
         functools.partial(y_kernel, n, nz),
         out_shape=(
             jax.ShapeDtypeStruct(adjoint.shape, f32),
             jax.ShapeDtypeStruct((2, fields, reach, rows, width), f32),
-            jax.ShapeDtypeStruct(adjoint.shape, f32),
         ),
         in_specs=[hbm, hbm, hbm, hbm, smem],
-        out_specs=(hbm, hbm, hbm),
+        out_specs=(hbm, hbm),
         scratch_shapes=[
             pltpu.VMEM((chunks, n, fields, rows, LANES), f32),
             pltpu.VMEM((half_n, planes, rows, width), f32),
@@ -398,20 +476,21 @@
             pltpu.VMEM((fields, depth + 2 * reach, TILE, width), f32),
             pltpu.VMEM((fields, depth, TILE, width), f32),
             pltpu.VMEM((depth, TILE, width), f32),
-            pltpu.VMEM((fields, depth, TILE, width), f32),
+            pltpu.VMEM(adjoint.shape, f32),
+            pltpu.VMEM(adjoint.shape, f32),
             dma((workers, chunks)), dma((half_n, chunks)),
             dma((half_n, chunks)), dma((half_n, chunks)),
             dma((half_n, 2)), dma((workers, chunks)),
-            dma((workers,)), dma((half_n,)),
-            dma((2,)), dma((2,)), dma((chunks,)), dma((2,)), dma((6,)),
+            dma((workers, chunks)), dma((half_n, chunks)),
+            dma((2, fields)), dma((2, fields)), dma((chunks,)), dma((2,)), dma((5,)), dma((workers, chunks)),
         ],
         compiler_params=pltpu.CompilerParams(
-            collective_id=0, has_side_effects=True, vmem_limit_bytes=56 * 2**20),
+            collective_id=0, has_side_effects=True, vmem_limit_bytes=58 * 2**20),
         cost_estimate=pl.CostEstimate(
             flops=12 * fields * depth * rows * width * extent,
             bytes_accessed=16 * fields * depth * rows * width, transcendentals=0),
     )(adjoint, speed, y_operators, x_derivative, jnp.transpose(coupling, (1, 0, 2)))
-    return local + terms
+    return out
 
 
 def solution(mesh):

time: 258 us -> 254 us (0.984)
  other arithmetic: 7.36 us -> 0 us
  local copies, waits for them, and re-layouts: 0 us -> 5.43 us
  Pallas kernels: 251 us -> 248 us
    add x1 -> x0, other arithmetic: 7.36 us -> none  [shards(): return local + terms]
    unnamed x0 -> x1, local copies, waits for them, and re-layouts: none -> 5.43 us
    pallas_call x1, Pallas kernels: 251 us -> 248 us  [shards(): pl.pallas_call(functools.partial(y_kernel, n, nz), out_shape=(jax.ShapeDt...]
where the time goes in v2:
time: 254 us
  Pallas kernels  248 us (98%)
  local copies, waits for them, and re-layouts  5.43 us (2%)
    pallas_call x1, Pallas kernels, shards(): pl.pallas_call(functools.partial(y_kernel, n, nz), out_shape=(jax.ShapeDt...  248 us
    unnamed x1, local copies, waits for them, and re-layouts  5.43 us

profile of v2, /device:TPU:1, one launch (start us, length us, event | category | flops | bytes accessed | tf_op | source)
XLA Modules:
  0.0 253.5 jit_solution(16241251399542190214)
XLA Ops:
  0.0 248.1 %shard_map.55 = (f32[5,8,128,256]{3,2,1,0:T(8,128)}, f32[2,5,4,128,256]{4,3,2,1,0:T(8,128)}) custom-call(f32[5,8,128,256]{3,2,1,0:T(8,128)} %adjoint.1, f32[8,128,256]{2,1,0:T(8,128)} %speed.1, f32[2,1024,1024]{2,1,0:T(8,128)} %y_ops.1, f32[256,256]{1,0:T(8,128)} %x_op.1, f32[5,3,5]{2,1,0:T(4,128)} %bitcast.1), custom_call_target="tpu_custom_call" | custom-call | flops 16106127360 | bytes 20971520 | tf_op jit(solution)/shard_map/pallas_call | solution.py:459
  248.1 5.4 %copy.7 = f32[5,8,128,256]{3,2,1,0:T(8,128)} copy(f32[5,8,128,256]{3,2,1,0:T(8,128)} %get-tuple-element.6) | data formatting | bytes 10485760
